TPU v7x, 512 devices: a whole 4x4x16 slice. The times are simulated.
512 devices in a mesh: dp: 16 (over z), head: 8 (over x, core), srv: 4 (over y).
Axes of the slice: x: 4, y: 4, z: 16, core: 2. Of those that a mesh axis runs over, the one named last changes fastest.
Arguments:
- queries: bfloat16 [2048, 8, 1024], P('dp', 'srv', 'head'), may hold values from -5 to 5
- keys: bfloat16 [10240, 1024], P(('dp', 'head')), may hold values from -5 to 5
- values: bfloat16 [10240, 1024], P(('dp', 'head')), may hold values from -6 to 6
- output_gradient: bfloat16 [2048, 8, 1024], P('dp', 'srv', 'head'), may hold values from -6 to 6
- doc_ids: int32 [10240], P('dp'), may hold values from 0 to 7, never falling along the last dimension, each value on 1 to 5120 neighbouring positions
Outputs:
- attention: bfloat16 [2048, 8, 1024], P('dp', 'srv', 'head')
- q_grad: bfloat16 [2048, 8, 1024], P('dp', 'srv', 'head')
- k_grad: bfloat16 [10240, 1024], P(('dp', 'head', 'srv'))
- v_grad: bfloat16 [10240, 1024], P(('dp', 'head', 'srv'))
Inputs may be any that keep to these rules, and one draw needn't show every extreme that they name: `doc_ids`: document numbers never fall along the keys; every document holds at most 5120 keys, and one holds exactly 5120.
All inputs are finite; a program needn't handle non-finite values.
Results may differ from a plain program's by a relative error of at most 0.039.
Values may be sent and summed in bfloat16 or wider, within the bound.
No kernel may reach another device: no remote copies, remote signals or barrier semaphores. Data moves between devices by JAX's collectives and lax.ppermute only.
A program may use at most 64 MiB of HBM per device.

v0:
```python
import math
import jax
import jax.numpy as jnp
from jax import lax
from jax.sharding import PartitionSpec as P

HEAD_SIZE = 128
NEGATIVE = -1e30


def local(queries, keys, values, output_gradient, doc_ids):
    home_rows, pair_heads, group_width = queries.shape
    groups = group_width // HEAD_SIZE
    scale_factor = HEAD_SIZE ** (-0.5)
    key_rows, value_rows = (
        lax.all_to_all(keys, "head", split_axis=1, concat_axis=0, tiled=True),
        lax.all_to_all(values, "head", split_axis=1, concat_axis=0, tiled=True),
    )
    key_count = key_rows.shape[0]
    servers = lax.axis_size("dp")
    server = lax.axis_index("dp")
    key_at = server * key_count + jnp.arange(key_count, dtype=jnp.int32)
    all_docs = lax.all_gather(doc_ids, "dp", axis=0, tiled=True)
    query_total = home_rows * servers
    context = all_docs.shape[0] - query_total
    query_docs = all_docs[context:]
    query_places = context + jnp.arange(query_total, dtype=jnp.int32)
    all_q, all_dout = (
        lax.all_gather(queries, "dp", axis=0, tiled=True),
        lax.all_gather(output_gradient, "dp", axis=0, tiled=True),
    )
    block_rows = math.gcd(512, query_total)
    block_count = query_total // block_rows
    key_heads = key_rows.reshape(key_count, groups, HEAD_SIZE)
    value_heads = value_rows.reshape(key_count, groups, HEAD_SIZE)
    query_blocks = all_q.reshape(block_count, block_rows, pair_heads, groups, HEAD_SIZE)
    grad_blocks = all_dout.reshape(block_count, block_rows, pair_heads, groups, HEAD_SIZE)
    place_blocks = query_places.reshape(block_count, block_rows)
    doc_blocks = query_docs.reshape(block_count, block_rows)

    def admissible(places, query_doc):
        return (key_at[None, :] <= places[:, None]) & (doc_ids[None, :] == query_doc[:, None])

    def scores_of(query_block):
        return (
            jnp.einsum("pjgd,kgd->gjpk", query_block, key_heads, preferred_element_type=jnp.float32)
            * scale_factor
        )

    def block_max(inputs):
        query_block, places, query_doc = inputs
        allowed = admissible(places, query_doc)

        def compute():
            raw_scores = scores_of(query_block)
            masked = jnp.where(allowed[None, None], raw_scores, NEGATIVE)
            return (jnp.max(masked, axis=-1).transpose(2, 1, 0), raw_scores)

        return compute()

    def block_top(inputs):
        return block_max(inputs)[0]

    local_max = lax.map(block_top, (query_blocks, place_blocks, doc_blocks))
    row_max = lax.pmax(local_max.reshape(query_total, pair_heads, groups), "dp")
    max_blocks = row_max.reshape(block_count, block_rows, pair_heads, groups)

    def block_sum(inputs):
        stored, places, query_doc, row_top = inputs
        allowed = admissible(places, query_doc)

        def compute():
            block_scores = scores_of(stored)
            shifted = block_scores - row_top.transpose(2, 1, 0)[..., None]
            weights = jnp.where(allowed[None, None], jnp.exp(shifted), 0.0)
            weighted = jnp.einsum(
                "gjpk,kgd->pjgd",
                weights.astype(jnp.bfloat16),
                value_heads,
                preferred_element_type=jnp.float32,
            )
            return (
                weighted.reshape(block_rows, pair_heads, group_width),
                jnp.sum(weights, axis=-1).transpose(2, 1, 0),
            )

        return compute()

    part_out, part_norm = lax.map(block_sum, (query_blocks, place_blocks, doc_blocks, max_blocks))
    part_out = part_out.reshape(query_total, pair_heads, group_width)
    part_norm = part_norm.reshape(query_total, pair_heads, groups)
    home_out, home_norm = (
        lax.psum_scatter(part_out, "dp", scatter_dimension=0, tiled=True),
        lax.psum_scatter(part_norm, "dp", scatter_dimension=0, tiled=True),
    )
    home_max = lax.dynamic_slice_in_dim(row_max, server * home_rows, home_rows, 0)
    attn_home = (
        home_out.reshape(home_rows, pair_heads, groups, HEAD_SIZE) / home_norm[..., None]
    ).astype(jnp.bfloat16)
    log_home = home_max + jnp.log(home_norm)
    grad_home = output_gradient.reshape(home_rows, pair_heads, groups, HEAD_SIZE).astype(
        jnp.float32
    )
    delta_home = jnp.sum(grad_home * attn_home.astype(jnp.float32), axis=-1)
    log_all, delta_all = (
        lax.all_gather(log_home, "dp", axis=0, tiled=True),
        lax.all_gather(delta_home, "dp", axis=0, tiled=True),
    )
    attention = attn_home.reshape(home_rows, pair_heads, group_width)
    log_blocks = log_all.reshape(block_count, block_rows, pair_heads, groups)
    delta_blocks = delta_all.reshape(block_count, block_rows, pair_heads, groups)

    def block_grad(totals, inputs):
        query_block, grad_block, places, query_doc, log_norm, row_delta = inputs
        allowed = admissible(places, query_doc)

        def compute():
            shifted = scores_of(query_block) - log_norm.transpose(2, 1, 0)[..., None]
            probs = jnp.where(allowed[None, None], jnp.exp(shifted), 0.0)
            value_grad = jnp.einsum(
                "gjpk,pjgd->kgd",
                probs.astype(jnp.bfloat16),
                grad_block,
                preferred_element_type=jnp.float32,
            )
            weight_grad = jnp.einsum(
                "pjgd,kgd->gjpk", grad_block, value_heads, preferred_element_type=jnp.float32
            )
            score_grad = (probs * (weight_grad - row_delta.transpose(2, 1, 0)[..., None])).astype(
                jnp.bfloat16
            )
            query_grad = (
                jnp.einsum(
                    "gjpk,kgd->pjgd", score_grad, key_heads, preferred_element_type=jnp.float32
                )
                * scale_factor
            )
            key_grad = (
                jnp.einsum(
                    "gjpk,pjgd->kgd", score_grad, query_block, preferred_element_type=jnp.float32
                )
                * scale_factor
            )
            return (query_grad.reshape(block_rows, pair_heads, group_width), key_grad, value_grad)

        query_grad, key_grad, value_grad = compute()
        return ((totals[0] + key_grad, totals[1] + value_grad), query_grad)

    zero_start = jnp.zeros((key_count, groups, HEAD_SIZE), jnp.float32)
    grad_inputs = (query_blocks, grad_blocks, place_blocks, doc_blocks, log_blocks, delta_blocks)
    (key_total, value_total), query_parts = lax.scan(
        block_grad, (zero_start, zero_start), grad_inputs
    )
    q_summed = lax.psum_scatter(
        query_parts.reshape(query_total, pair_heads, group_width).astype(jnp.bfloat16),
        "dp",
        scatter_dimension=0,
        tiled=True,
    )
    spread_key, spread_value = (
        lax.all_to_all(
            key_total.reshape(key_count, group_width).astype(jnp.bfloat16),
            "head",
            split_axis=0,
            concat_axis=1,
            tiled=True,
        ).astype(jnp.float32),
        lax.all_to_all(
            value_total.reshape(key_count, group_width).astype(jnp.bfloat16),
            "head",
            split_axis=0,
            concat_axis=1,
            tiled=True,
        ).astype(jnp.float32),
    )
    k_summed, v_summed = (
        lax.psum_scatter(
            spread_key.astype(jnp.bfloat16), "srv", scatter_dimension=0, tiled=True
        ).astype(jnp.float32),
        lax.psum_scatter(
            spread_value.astype(jnp.bfloat16), "srv", scatter_dimension=0, tiled=True
        ).astype(jnp.float32),
    )
    return (attention, q_summed, k_summed.astype(jnp.bfloat16), v_summed.astype(jnp.bfloat16))


def solution(mesh):
    placed = (
        P("dp", "srv", "head"),
        P(("dp", "head"), None),
        P(("dp", "head"), None),
        P("dp", "srv", "head"),
        P("dp"),
    )
    return jax.shard_map(
        local,
        mesh=mesh,
        in_specs=placed,
        out_specs=(
            P("dp", "srv", "head"),
            P("dp", "srv", "head"),
            P(("dp", "head", "srv"), None),
            P(("dp", "head", "srv"), None),
        ),
        check_vma=False,
    )
```

profile of v0, /device:TPU:2, one launch (start us, length us, event | category | flops | bytes accessed | tf_op | source)
XLA Modules:
  0.0 651.0 jit_solution(6897663471784736279)
XLA Ops:
  7.2 1.5 copy.61
  9.5 9.2 %all-to-all-start = ((bf16[80,8,128]{2,0,1:T(8,128)(2,1)}), bf16[80,8,128]{2,0,1:T(8,128)(2,1)S(1)}, u32[]{:S(2)}, u32[]{:S(2)}) async-start(bf16[80,8,128]{2,0,1:T(8,128)(2,1)} %copy_bitcast_fusion.3), calls=%async_computation | async-start | bytes 327680 | tf_op jit(solution)/shard_map/all_to_all | solution.py:16
  18.7 1.6 copy_bitcast_fusion.2
  21.0 31.2 %all-gather.1 = s32[16,1,640]{2,1,0:T(1,128)S(1)} all-gather(s32[1,1,640]{2,1,0:T(1,128)S(1)} %reshape.364), channel_id=1, replica_groups=mesh['dp'=16,'head'=8,'srv'=4] {'dp'}, dimensions={0}, use_global_device_ids=true | all-gather | bytes 43520 | tf_op jit(solution)/shard_map/all_gather | solution.py:23
  52.8 33.4 %all-gather.5.cloned.1.call-done = bf16[2048,2,128]{2,0,1:T(8,128)(2,1)} async-done(((bf16[128,2,128]{2,0,1:T(8,128)(2,1)}), bf16[2048,2,128]{2,0,1:T(8,128)(2,1)}) %all-gather.5.cloned.1.call-update) | async-done | bytes 1048592 | tf_op jit(solution)/shard_map/all_gather | solution.py:29
  86.3 1.3 copy.66
  87.6 4.8 all-to-all-start.1
  92.4 7.6 %while.39 = (s32[]{:T(128)}, f32[4,512,2,1]{1,0,2,3:T(4,128)S(1)}, s32[4,512]{1,0:T(4,128)}, s32[640]{0:T(1024)S(1)}, s32[4,512]{1,0:T(4,128)S(1)}, /*index=5*/b...) while((s32[]{:T(128)}, f32[4,512,2,1]{1,0,2,3:T(4,128)S(1)}, ...), condition=%wide.region_2.3_spmd.clone, body=%wide.region_0.2_spmd.clone.sunk | while | flops 170720896 | bytes 1121917 | solution.py:64
  92.4 0.7 constant_dynamic-slice_fusion.12
  93.5 0.8 fusion.104
  94.3 0.7 constant_dynamic-slice_fusion.12
  95.4 0.8 fusion.104
  96.2 0.7 constant_dynamic-slice_fusion.12
  97.3 0.8 fusion.104
  99.2 0.8 fusion.104
  100.0 55.1 %pmax.7 = f32[2048,2,1]{0,1,2:T(2,128)} all-reduce(f32[2048,2,1]{0,1,2:T(2,128)S(1)} %reshape.354), channel_id=1, replica_groups=mesh['dp'=16,'head'=8,'srv'=4] {'dp'}, use_global_device_ids=true, to_apply=%region_3.4 | all-reduce | flops 4096 | bytes 32768 | tf_op jit(solution)/shard_map/pmax | solution.py:65
  155.1 22.3 %while.40 = (s32[]{:T(128)}, f32[4,512,2,128]{3,2,1,0:T(2,128)S(1)}, f32[4,512,2,1]{1,3,2,0:T(1,128)}, s32[4,512]{1,0:T(4,128)}, s32[640]{0:T(1024)S(1)}, /*inde...) while((s32[]{:T(128)}, ...), condition=%wide.region_6.7_spmd.clone, body=%wide.region_4.6_spmd.clone.sunk | while | flops 341769856 | bytes 8437397 | solution.py:89
  156.9 1.1 fusion.107
  157.9 1.7 fusion.108
  162.4 1.0 fusion.107
  163.5 1.7 fusion.108
  168.0 1.0 fusion.107
  169.1 1.7 fusion.108
  173.6 1.0 fusion.107
  174.6 1.7 fusion.108
  177.4 2.1 copy.88
  181.1 1.3 dynamic-slice
  183.0 63.6 %reduce-scatter.8.cloned.1.call-done = f32[128,2]{1,0:T(8,128)} async-done(((f32[2048,2]{1,0:T(8,128)}), f32[128,2]{1,0:T(8,128)}) %reduce-scatter.8.cloned.1.call-update) | async-done | bytes 1040
  246.6 0.9 copy.87
  248.3 27.4 %all_gather.17 = f32[2048,2,1]{0,1,2:T(2,128)S(1)} all-gather(f32[128,2,1]{0,1,2:T(2,128)S(1)} %log_add_fusion), channel_id=1, replica_groups=mesh['dp'=16,'head'=8,'srv'=4] {'dp'}, dimensions={0}, use_global_device_ids=true | all-gather | bytes 17408 | tf_op jit(solution)/shard_map/all_gather | solution.py:106
  275.7 115.2 %all-reduce.10.cloned.1.call-done = f32[2048,2,128]{2,1,0:T(2,128)} async-done(((f32[2048,2,128]{2,1,0:T(2,128)}), f32[2048,2,128]{2,1,0:T(2,128)}) %all-reduce.10.cloned.1.call-update) | async-done | bytes 2097168
  390.9 1.7 multiply_reduce_fusion
  392.6 35.8 %all-gather = f32[2048,2]{1,0:T(8,128)S(1)} all-gather(f32[128,2]{1,0:T(8,128)S(1)} %get-tuple-element.445), channel_id=2, replica_groups=mesh['dp'=16,'head'=8,'srv'=4] {'dp'}, dimensions={0}, use_global_device_ids=true | all-gather | bytes 17408 | tf_op jit(solution)/shard_map/all_gather | solution.py:107
  428.7 32.1 %all-gather.7.cloned.1.call-done = bf16[2048,2,128]{2,0,1:T(8,128)(2,1)} async-done(((bf16[128,2,128]{2,0,1:T(8,128)(2,1)}), bf16[2048,2,128]{2,0,1:T(8,128)(2,1)}) %all-gather.7.cloned.1.call-update) | async-done | bytes 1048592 | tf_op jit(solution)/shard_map/all_gather | solution.py:30
  460.8 37.4 %while.41 = (s32[]{:T(128)}, f32[640,1,128]{0,2,1:T(8,128)S(1)}, f32[640,1,128]{0,2,1:T(8,128)}, bf16[4,512,2,128]{3,1,2,0:T(8,128)(2,1)}, bf16[4,512,2,1,128]{4...) while((s32[]{:T(128)}, f32[640,1,128]{0,2,1:T(8,128)S(1)}, ...), condition=%wide.region_11.12_spmd.clone, body=%wide.region_10.11_spmd.clone.sunk | while | flops 846938752 | bytes 35077916 | solution.py:151
  461.4 0.8 constant_dynamic-slice_fusion.14
  462.5 2.0 fusion.120
  465.0 3.6 fusion.122
  469.2 1.0 copy-done.5
  470.7 0.8 constant_dynamic-slice_fusion.14
  471.8 2.0 fusion.120
  474.4 3.6 fusion.122
  478.5 1.0 copy-done.5
  480.1 0.8 constant_dynamic-slice_fusion.14
  481.1 2.0 fusion.120
  483.7 3.6 fusion.122
  487.9 1.0 copy-done.5
  489.4 0.8 constant_dynamic-slice_fusion.14
  490.5 2.0 fusion.120
  493.1 3.6 fusion.122
  497.2 1.0 copy-done.5
  498.2 0.8 copy.78
  499.0 4.9 all-to-all-start.2
  503.9 3.3 copy.77
  507.2 0.8 copy.80
  508.0 0.9 all-to-all-done.2
  508.9 4.8 all-to-all-start.3
  513.7 5.0 all-to-all-done.3
  518.8 12.6 %fusion.72 = (bf16[24,1024]{1,0:T(8,128)(2,1)S(1)}, bf16[24,1024]{1,0:T(8,128)(2,1)S(1)}) fusion(bf16[80,1024]{1,0:T(8,128)(2,1)S(1)} %copy_bitcast_fusion.1, bf16[80,1024]{1,0:T(8,128)(2,1)S(1)} %copy_bitcast_fusion), kind=kCustom, calls=%all-reduce-scatter.2 | all-reduce-scatter fusion | flops 196609 | bytes 428032
  531.4 1.6 collective-permute-start
  533.0 3.1 collective-permute-start.1
  536.0 1.3 dynamic-slice.10
  539.6 103.4 %all-reduce.12.cloned.1.call-done = bf16[2048,2,128]{2,1,0:T(2,128)(2,1)} async-done(((bf16[2048,2,128]{2,1,0:T(2,128)(2,1)}), bf16[2048,2,128]{2,1,0:T(2,128)(2,1)}) %all-reduce.12.cloned.1.call-update) | async-done | bytes 1048592
  643.0 1.5 constant_dynamic-slice_fusion.8
  (133 shorter events, 27.3 us)
Async XLA Ops:
  7.2 1.6 copy-start
  7.2 85.2 %copy-start.3 = (s32[640]{0:T(1024)S(1)}, s32[640]{0:T(1024)}, u32[]{:S(2)}) copy-start(s32[640]{0:T(1024)} %param.15) | copy-start | bytes 7684
  7.2 79.1 %all-gather.5.cloned.1.call-start = ((), (), s32[]{:S(2)}) async-start(), calls=%async_computation.5 | async-start | bytes 1114112 | tf_op jit(solution)/shard_map/all_gather | solution.py:29
  9.5 78.1 %all-to-all-start = ((bf16[80,8,128]{2,0,1:T(8,128)(2,1)}), bf16[80,8,128]{2,0,1:T(8,128)(2,1)S(1)}, u32[]{:S(2)}, u32[]{:S(2)}) async-start(bf16[80,8,128]{2,0,1:T(8,128)(2,1)} %copy_bitcast_fusion.3), calls=%async_computation | async-start | bytes 327680 | tf_op jit(solution)/shard_map/all_to_all | solution.py:16
  87.6 67.6 %all-to-all-start.1 = ((bf16[80,8,128]{2,0,1:T(8,128)(2,1)}), bf16[80,8,128]{2,0,1:T(8,128)(2,1)}, u32[]{:S(2)}, u32[]{:S(2)}) async-start(bf16[80,8,128]{2,0,1:T(8,128)(2,1)} %copy_bitcast_fusion.2), calls=%async_computation.1 | async-start | bytes 327680 | tf_op jit(solution)/shard_map/all_to_all | solution.py:17
  92.4 154.2 %reduce-scatter.8.cloned.1.call-start = ((), (), s32[]{:S(2)}) async-start(), calls=%async_computation.7 | async-start | bytes 1114112
  177.4 2.2 copy-start.2
  177.4 2.9 copy-start.7
  179.6 211.3 %all-reduce.10.cloned.1.call-start = ((), (), s32[]{:S(2)}) async-start(), calls=%async_computation.8 | async-start | bytes 4194304
  180.3 280.5 %all-gather.7.cloned.1.call-start = ((), (), s32[]{:S(2)}) async-start(), calls=%async_computation.6 | async-start | bytes 1114112 | tf_op jit(solution)/shard_map/all_gather | solution.py:30
  461.3 3.2 copy-start.1
  465.0 3.6 copy-start.4
  469.2 1.0 copy-start.5
  470.7 3.2 copy-start.1
  474.4 3.6 copy-start.4
  478.5 1.0 copy-start.5
  480.0 3.2 copy-start.1
  483.7 3.6 copy-start.4
  487.9 1.0 copy-start.5
  489.4 3.2 copy-start.1
  493.1 3.6 copy-start.4
  497.2 1.0 copy-start.5
  498.2 9.0 %copy-start.6 = (f32[640,1,128]{0,2,1:T(8,128)S(1)}, f32[640,1,128]{0,2,1:T(8,128)}, u32[]{:S(2)}) copy-start(f32[640,1,128]{0,2,1:T(8,128)} %get-tuple-element.183) | copy-start | bytes 983044
  499.0 9.9 %all-to-all-start.2 = ((bf16[8,80,128]{2,1,0:T(8,128)(2,1)}), bf16[8,80,128]{2,1,0:T(8,128)(2,1)S(1)}, u32[]{:S(2)}, u32[]{:S(2)}) async-start(bf16[8,80,128]{2,1,0:T(8,128)(2,1)} %bitcast.15), calls=%async_computation.2 | async-start | bytes 327680 | tf_op jit(solution)/shard_map/all_to_all | solution.py:161
  503.9 139.1 %all-reduce.12.cloned.1.call-start = ((), (), s32[]{:S(2)}) async-start(), calls=%async_computation.9 | async-start | bytes 2097152
  508.9 9.8 %all-to-all-start.3 = ((bf16[8,80,128]{2,1,0:T(8,128)(2,1)}), bf16[8,80,128]{2,1,0:T(8,128)(2,1)S(1)}, u32[]{:S(2)}, u32[]{:S(2)}) async-start(bf16[8,80,128]{2,1,0:T(8,128)(2,1)} %bitcast.17), calls=%async_computation.3 | async-start | bytes 327680 | tf_op jit(solution)/shard_map/all_to_all | solution.py:168
  531.4 6.6 %collective-permute-start = (bf16[12,1024]{1,0:T(8,128)(2,1)S(1)}, bf16[12,1024]{1,0:T(8,128)(2,1)S(1)}, u32[]{:S(2)}, u32[]{:S(2)}) collective-permute-start(bf16[12,1024]{1,0:T(8,128)(2,1)S(1)} %slice.16), channel_id=1, source_target_pairs={{0,1},{1,2},{2,3},{4,5},{5,6},{6,7},{8,9},{9,10},{10,11},{12,13},{... | collective-permute-start | bytes 73736
  533.0 5.2 collective-permute-start.1
Sparse Core Ops, SparseCore 0:
  10.7 75.5 all-gather.4
  179.7 66.8 reduce-scatter.7
  249.1 141.7 all-reduce.9
  393.6 67.1 all-gather.6
  507.3 135.5 all-reduce.11
where the time goes:
time: 653 us; the launch traced here: 651 us
  waiting for transfers between devices  354 us (54%)
  blocking collectives  162 us (25%)
  matrix products  42.8 us (7%)
  local copies, waits for them, and re-layouts  40.5 us (6%)
  starting transfers between devices  28.4 us (4%)
  between operations  15.3 us (2%)
  other arithmetic  7 us (1%)
    unnamed x10, waiting for transfers between devices  283 us
    pmax x1, blocking collectives, local(): row_max = lax.pmax(local_max.reshape(query_total, pair_heads, groups), 'dp')  55.1 us
    all_gather x1, blocking collectives, local(): lax.all_gather(delta_home, 'dp', axis=0, tiled=True)  35.8 us
    all_gather x1, waiting for transfers between devices, local(): lax.all_gather(queries, 'dp', axis=0, tiled=True)  33.4 us
    all_gather x1, waiting for transfers between devices, local(): lax.all_gather(output_gradient, 'dp', axis=0, tiled=True)  32.1 us
    all_gather x1, blocking collectives, local(): all_docs = lax.all_gather(doc_ids, 'dp', axis=0, tiled=True)  31.2 us
    all_gather x1, blocking collectives, local(): lax.all_gather(log_home, 'dp', axis=0, tiled=True)  27.4 us
    dot_general x4, matrix products, compute(): jnp.einsum('gjpk,pjgd->kgd', probs.astype(jnp.bfloat16), grad_block, pref...  14.3 us
  transfers between devices with their start and end apart: 11, of which 7 were waited for; matrix products, arithmetic and copies ran while one was open for 6% of the time, Pallas kernels for 0%

commit v1 on v0

--- a/solution.py
+++ b/solution.py
@@ -6,6 +6,27 @@
 
 HEAD_SIZE = 128
 NEGATIVE = -1e30
+
+
+def joined_along(blocks, dim):
+    shape = list(blocks.shape[1:])
+    shape[dim] *= blocks.shape[0]
+    return jnp.moveaxis(blocks, 0, dim).reshape(shape)
+
+
+def grow_blocks(array, axis):
+    count, index = (lax.axis_size(axis), lax.axis_index(axis))
+    blocks, apart = (array[None], 1)
+    while apart < count:
+        other = lax.ppermute(blocks, axis, [(i, i ^ apart) for i in range(count)])
+        low = index & apart == 0
+        blocks = jnp.concatenate([jnp.where(low, blocks, other), jnp.where(low, other, blocks)])
+        apart *= 2
+    return blocks
+
+
+def collect(shard, axis, dim):
+    return joined_along(grow_blocks(shard, axis), dim)
 
 
 def local(queries, keys, values, output_gradient, doc_ids):
@@ -103,7 +124,7 @@
     )
     delta_home = jnp.sum(grad_home * attn_home.astype(jnp.float32), axis=-1)
     log_all, delta_all = (
-        lax.all_gather(log_home, "dp", axis=0, tiled=True),
+        collect(log_home, "dp", 0),
         lax.all_gather(delta_home, "dp", axis=0, tiled=True),
     )
     attention = attn_home.reshape(home_rows, pair_heads, group_width)

time: 653 us -> 653 us (level)
  blocking collectives: 162 us -> 135 us
  starting transfers between devices: 28.4 us -> 49.7 us
  waiting for transfers between devices: 354 us -> 361 us
    all_gather x1 -> x0, blocking collectives: 27.4 us -> none  [local(): lax.all_gather(log_home, 'dp', axis=0, tiled=True)]
    ppermute x0 -> x4, starting transfers between devices: none -> 21.4 us  [grow_blocks(): other = lax.ppermute(blocks, axis, [(i, i ^ apart) for i in range(count)])]
    ppermute x0 -> x4, waiting for transfers between devices: none -> 12.2 us  [grow_blocks(): other = lax.ppermute(blocks, axis, [(i, i ^ apart) for i in range(count)])]
  transfers between devices with their start and end apart: 11 -> 15, of which waited for: 7 -> 11; matrix products, arithmetic and copies ran while one was open for 6% -> 6% of each run, Pallas kernels for 0% -> 0%
where the time goes in v1:
time: 653 us; the launch traced here: 651 us
  waiting for transfers between devices  361 us (55%)
  blocking collectives  135 us (21%)
  starting transfers between devices  49.7 us (8%)
  matrix products  42.9 us (7%)
  local copies, waits for them, and re-layouts  40.4 us (6%)
  between operations  15.3 us (2%)
  other arithmetic  7.07 us (1%)
    unnamed x10, waiting for transfers between devices  277 us
    pmax x1, blocking collectives, local(): row_max = lax.pmax(local_max.reshape(query_total, pair_heads, groups), 'dp')  55.1 us
    all_gather x1, blocking collectives, local(): lax.all_gather(delta_home, 'dp', axis=0, tiled=True)  35.7 us
    all_gather x1, waiting for transfers between devices, local(): lax.all_gather(queries, 'dp', axis=0, tiled=True)  33.5 us
    all_gather x1, waiting for transfers between devices, local(): lax.all_gather(output_gradient, 'dp', axis=0, tiled=True)  32.2 us
    all_gather x1, blocking collectives, local(): all_docs = lax.all_gather(doc_ids, 'dp', axis=0, tiled=True)  31.2 us
    ppermute x4, starting transfers between devices, grow_blocks(): other = lax.ppermute(blocks, axis, [(i, i ^ apart) for i in range(count)])  21.4 us
    dot_general x4, matrix products, compute(): jnp.einsum('gjpk,pjgd->kgd', probs.astype(jnp.bfloat16), grad_block, pref...  14.3 us
  transfers between devices with their start and end apart: 15, of which 11 were waited for; matrix products, arithmetic and copies ran while one was open for 6% of the time, Pallas kernels for 0%

profile of v1, /device:TPU:2, one launch (start us, length us, event | category | flops | bytes accessed | tf_op | source)
XLA Modules:
  0.0 651.2 jit_solution(15184315082875059079)
XLA Ops:
  7.2 1.5 copy.63
  9.5 9.2 %all-to-all-start = ((bf16[80,8,128]{2,0,1:T(8,128)(2,1)}), bf16[80,8,128]{2,0,1:T(8,128)(2,1)S(1)}, u32[]{:S(2)}, u32[]{:S(2)}) async-start(bf16[80,8,128]{2,0,1:T(8,128)(2,1)} %copy_bitcast_fusion.3), calls=%async_computation | async-start | bytes 327680 | tf_op jit(solution)/shard_map/all_to_all | solution.py:37
  18.7 1.6 copy_bitcast_fusion.2
  21.0 31.2 %all-gather.1 = s32[16,1,640]{2,1,0:T(1,128)S(1)} all-gather(s32[1,1,640]{2,1,0:T(1,128)S(1)} %reshape.360), channel_id=1, replica_groups=mesh['dp'=16,'head'=8,'srv'=4] {'dp'}, dimensions={0}, use_global_device_ids=true | all-gather | bytes 43520 | tf_op jit(solution)/shard_map/all_gather | solution.py:44
  52.8 33.5 %all-gather.5.cloned.1.call-done = bf16[2048,2,128]{2,0,1:T(8,128)(2,1)} async-done(((bf16[128,2,128]{2,0,1:T(8,128)(2,1)}), bf16[2048,2,128]{2,0,1:T(8,128)(2,1)}) %all-gather.5.cloned.1.call-update) | async-done | bytes 1048592 | tf_op jit(solution)/shard_map/all_gather | solution.py:50
  86.3 1.3 copy.68
  87.6 4.8 all-to-all-start.1
  92.4 7.6 %while.39 = (s32[]{:T(128)}, f32[4,512,2,1]{1,0,2,3:T(4,128)S(1)}, s32[4,512]{1,0:T(4,128)}, s32[640]{0:T(1024)S(1)}, s32[4,512]{1,0:T(4,128)S(1)}, /*index=5*/b...) while((s32[]{:T(128)}, f32[4,512,2,1]{1,0,2,3:T(4,128)S(1)}, ...), condition=%wide.region_2.3_spmd.clone, body=%wide.region_0.2_spmd.clone.sunk | while | flops 170720896 | bytes 1121917 | solution.py:85
  93.5 0.8 fusion.104
  95.4 0.8 fusion.104
  97.3 0.8 fusion.104
  99.2 0.8 fusion.104
  100.0 55.1 %pmax.7 = f32[2048,2,1]{0,1,2:T(2,128)} all-reduce(f32[2048,2,1]{0,1,2:T(2,128)S(1)} %reshape.351), channel_id=1, replica_groups=mesh['dp'=16,'head'=8,'srv'=4] {'dp'}, use_global_device_ids=true, to_apply=%region_3.4 | all-reduce | flops 4096 | bytes 32768 | tf_op jit(solution)/shard_map/pmax | solution.py:86
  155.2 22.3 %while.40 = (s32[]{:T(128)}, f32[4,512,2,128]{3,2,1,0:T(2,128)S(1)}, f32[4,512,2,1]{1,3,2,0:T(1,128)}, s32[4,512]{1,0:T(4,128)}, s32[640]{0:T(1024)S(1)}, /*inde...) while((s32[]{:T(128)}, ...), condition=%wide.region_6.7_spmd.clone, body=%wide.region_4.6_spmd.clone.sunk | while | flops 341769856 | bytes 8437397 | solution.py:110
  156.9 1.0 fusion.107
  158.0 1.7 fusion.108
  162.5 1.0 fusion.107
  163.5 1.7 fusion.108
  168.1 1.1 fusion.107
  169.1 1.7 fusion.108
  173.6 1.0 fusion.107
  174.7 1.7 fusion.108
  177.5 2.1 copy.91
  181.1 65.4 %reduce-scatter.8.cloned.1.call-done = f32[128,2]{1,0:T(8,128)} async-done(((f32[2048,2]{1,0:T(8,128)}), f32[128,2]{1,0:T(8,128)}) %reduce-scatter.8.cloned.1.call-update) | async-done | bytes 1040
  246.6 0.9 copy.90
  248.2 2.9 collective-permute-start
  251.1 2.5 collective-permute-done
  253.6 3.6 collective-permute-start.1
  257.2 2.8 collective-permute-done.1
  260.0 5.7 collective-permute-start.2
  265.8 3.8 collective-permute-done.2
  269.5 9.1 %collective-permute-start.3 = (f32[8,128,2,1]{1,2,3,0:T(2,128)S(1)}, f32[8,128,2,1]{1,2,3,0:T(2,128)S(1)}, u32[]{:S(2)}, u32[]{:S(2)}) collective-permute-start(f32[8,128,2,1]{1,2,3,0:T(2,128)S(1)} %pad_maximum_fusion.1), channel_id=1, source_target_pairs={{0,256},{32,288},{64,320},{96,352},{128,384},{160,416},{192,448},{... | collective-permute-start | bytes 24584 | tf_op jit(solution)/shard_map/ppermute | solution.py:21
  278.7 1.3 dynamic-slice
  280.7 3.2 collective-permute-done.3
  284.0 107.2 %all-reduce.10.cloned.1.call-done = f32[2048,2,128]{2,1,0:T(2,128)} async-done(((f32[2048,2,128]{2,1,0:T(2,128)}), f32[2048,2,128]{2,1,0:T(2,128)}) %all-reduce.10.cloned.1.call-update) | async-done | bytes 2097168
  391.1 1.7 multiply_reduce_fusion
  392.9 35.7 %all-gather = f32[2048,2]{1,0:T(8,128)S(1)} all-gather(f32[128,2]{1,0:T(8,128)S(1)} %get-tuple-element.445), channel_id=2, replica_groups=mesh['dp'=16,'head'=8,'srv'=4] {'dp'}, dimensions={0}, use_global_device_ids=true | all-gather | bytes 17408 | tf_op jit(solution)/shard_map/all_gather | solution.py:128
  428.9 32.2 %all-gather.7.cloned.1.call-done = bf16[2048,2,128]{2,0,1:T(8,128)(2,1)} async-done(((bf16[128,2,128]{2,0,1:T(8,128)(2,1)}), bf16[2048,2,128]{2,0,1:T(8,128)(2,1)}) %all-gather.7.cloned.1.call-update) | async-done | bytes 1048592 | tf_op jit(solution)/shard_map/all_gather | solution.py:51
  461.2 37.3 %while.41 = (s32[]{:T(128)}, f32[640,1,128]{0,2,1:T(8,128)S(1)}, f32[640,1,128]{0,2,1:T(8,128)}, bf16[4,512,2,128]{3,1,2,0:T(8,128)(2,1)}, bf16[4,512,2,1,128]{4...) while((s32[]{:T(128)}, f32[640,1,128]{0,2,1:T(8,128)S(1)}, ...), condition=%wide.region_11.12_spmd.clone, body=%wide.region_10.11_spmd.clone.sunk | while | flops 846938752 | bytes 35077916 | solution.py:172
  462.8 2.0 fusion.120
  465.4 3.6 fusion.122
  469.5 1.0 copy-done.5
  472.1 2.0 fusion.120
  474.7 3.6 fusion.122
  478.9 1.0 copy-done.5
  481.4 2.0 fusion.120
  484.0 3.6 fusion.122
  488.2 1.0 copy-done.5
  490.8 2.0 fusion.120
  493.4 3.6 fusion.122
  497.5 1.0 copy-done.5
  498.5 0.8 copy.81
  499.3 4.8 all-to-all-start.2
  504.1 3.3 copy.80
  507.5 0.8 copy.83
  508.3 0.9 all-to-all-done.2
  509.1 4.8 all-to-all-start.3
  513.9 5.0 all-to-all-done.3
  519.0 12.6 %fusion.72 = (bf16[24,1024]{1,0:T(8,128)(2,1)S(1)}, bf16[24,1024]{1,0:T(8,128)(2,1)S(1)}) fusion(bf16[80,1024]{1,0:T(8,128)(2,1)S(1)} %copy_bitcast_fusion.1, bf16[80,1024]{1,0:T(8,128)(2,1)S(1)} %copy_bitcast_fusion), kind=kCustom, calls=%all-reduce-scatter.2 | all-reduce-scatter fusion | flops 196609 | bytes 428032
  531.6 1.6 collective-permute-start.4
  533.2 3.1 collective-permute-start.5
  536.2 1.3 dynamic-slice.10
  539.8 103.3 %all-reduce.12.cloned.1.call-done = bf16[2048,2,128]{2,1,0:T(2,128)(2,1)} async-done(((bf16[2048,2,128]{2,1,0:T(2,128)(2,1)}), bf16[2048,2,128]{2,1,0:T(2,128)(2,1)}) %all-reduce.12.cloned.1.call-update) | async-done | bytes 1048592
  643.1 1.5 constant_dynamic-slice_fusion.8
  (148 shorter events, 32.5 us)
Async XLA Ops:
  7.2 1.6 copy-start
  7.2 85.2 %copy-start.3 = (s32[640]{0:T(1024)S(1)}, s32[640]{0:T(1024)}, u32[]{:S(2)}) copy-start(s32[640]{0:T(1024)} %param.15) | copy-start | bytes 7684
  7.2 79.1 %all-gather.5.cloned.1.call-start = ((), (), s32[]{:S(2)}) async-start(), calls=%async_computation.5 | async-start | bytes 1114112 | tf_op jit(solution)/shard_map/all_gather | solution.py:50
  9.5 78.1 %all-to-all-start = ((bf16[80,8,128]{2,0,1:T(8,128)(2,1)}), bf16[80,8,128]{2,0,1:T(8,128)(2,1)S(1)}, u32[]{:S(2)}, u32[]{:S(2)}) async-start(bf16[80,8,128]{2,0,1:T(8,128)(2,1)} %copy_bitcast_fusion.3), calls=%async_computation | async-start | bytes 327680 | tf_op jit(solution)/shard_map/all_to_all | solution.py:37
  87.6 67.6 %all-to-all-start.1 = ((bf16[80,8,128]{2,0,1:T(8,128)(2,1)}), bf16[80,8,128]{2,0,1:T(8,128)(2,1)}, u32[]{:S(2)}, u32[]{:S(2)}) async-start(bf16[80,8,128]{2,0,1:T(8,128)(2,1)} %copy_bitcast_fusion.2), calls=%async_computation.1 | async-start | bytes 327680 | tf_op jit(solution)/shard_map/all_to_all | solution.py:38
  92.4 154.2 %reduce-scatter.8.cloned.1.call-start = ((), (), s32[]{:S(2)}) async-start(), calls=%async_computation.7 | async-start | bytes 1114112
  177.5 2.2 copy-start.2
  177.5 2.9 copy-start.7
  179.6 211.5 %all-reduce.10.cloned.1.call-start = ((), (), s32[]{:S(2)}) async-start(), calls=%async_computation.8 | async-start | bytes 4194304
  180.4 280.8 %all-gather.7.cloned.1.call-start = ((), (), s32[]{:S(2)}) async-start(), calls=%async_computation.6 | async-start | bytes 1114112 | tf_op jit(solution)/shard_map/all_gather | solution.py:51
  248.2 5.5 collective-permute-start
  253.6 6.4 collective-permute-start.1
  260.0 9.5 %collective-permute-start.2 = (f32[4,128,2,1]{1,2,3,0:T(2,128)S(1)}, f32[4,128,2,1]{1,2,3,0:T(2,128)S(1)}, u32[]{:S(2)}, u32[]{:S(2)}) collective-permute-start(f32[4,128,2,1]{1,2,3,0:T(2,128)S(1)} %pad_maximum_fusion.2), channel_id=1, source_target_pairs={{0,128},{32,160},{64,192},{96,224},{128,0},{160,32},{192,64},{224,... | collective-permute-start | bytes 12296 | tf_op jit(solution)/shard_map/ppermute | solution.py:21
  269.5 14.4 %collective-permute-start.3 = (f32[8,128,2,1]{1,2,3,0:T(2,128)S(1)}, f32[8,128,2,1]{1,2,3,0:T(2,128)S(1)}, u32[]{:S(2)}, u32[]{:S(2)}) collective-permute-start(f32[8,128,2,1]{1,2,3,0:T(2,128)S(1)} %pad_maximum_fusion.1), channel_id=1, source_target_pairs={{0,256},{32,288},{64,320},{96,352},{128,384},{160,416},{192,448},{... | collective-permute-start | bytes 24584 | tf_op jit(solution)/shard_map/ppermute | solution.py:21
  461.7 3.2 copy-start.1
  465.4 3.6 copy-start.4
  469.5 1.0 copy-start.5
  471.0 3.2 copy-start.1
  474.7 3.6 copy-start.4
  478.8 1.0 copy-start.5
  480.3 3.2 copy-start.1
  484.0 3.6 copy-start.4
  488.2 1.0 copy-start.5
  489.7 3.2 copy-start.1
  493.4 3.6 copy-start.4
  497.5 1.0 copy-start.5
  498.5 8.9 %copy-start.6 = (f32[640,1,128]{0,2,1:T(8,128)S(1)}, f32[640,1,128]{0,2,1:T(8,128)}, u32[]{:S(2)}) copy-start(f32[640,1,128]{0,2,1:T(8,128)} %get-tuple-element.183) | copy-start | bytes 983044
  499.3 9.8 %all-to-all-start.2 = ((bf16[8,80,128]{2,1,0:T(8,128)(2,1)}), bf16[8,80,128]{2,1,0:T(8,128)(2,1)S(1)}, u32[]{:S(2)}, u32[]{:S(2)}) async-start(bf16[8,80,128]{2,1,0:T(8,128)(2,1)} %bitcast.16), calls=%async_computation.2 | async-start | bytes 327680 | tf_op jit(solution)/shard_map/all_to_all | solution.py:182
  504.1 139.0 %all-reduce.12.cloned.1.call-start = ((), (), s32[]{:S(2)}) async-start(), calls=%async_computation.9 | async-start | bytes 2097152
  509.1 9.8 %all-to-all-start.3 = ((bf16[8,80,128]{2,1,0:T(8,128)(2,1)}), bf16[8,80,128]{2,1,0:T(8,128)(2,1)S(1)}, u32[]{:S(2)}, u32[]{:S(2)}) async-start(bf16[8,80,128]{2,1,0:T(8,128)(2,1)} %bitcast.18), calls=%async_computation.3 | async-start | bytes 327680 | tf_op jit(solution)/shard_map/all_to_all | solution.py:189
  531.6 6.6 %collective-permute-start.4 = (bf16[12,1024]{1,0:T(8,128)(2,1)S(1)}, bf16[12,1024]{1,0:T(8,128)(2,1)S(1)}, u32[]{:S(2)}, u32[]{:S(2)}) collective-permute-start(bf16[12,1024]{1,0:T(8,128)(2,1)S(1)} %slice.16), channel_id=1, source_target_pairs={{0,1},{1,2},{2,3},{4,5},{5,6},{6,7},{8,9},{9,10},{10,11},{12,13},{... | collective-permute-start | bytes 73736
  533.2 5.2 collective-permute-start.5
Sparse Core Ops, SparseCore 0:
  10.7 75.5 all-gather.4
  179.8 66.7 reduce-scatter.7
  249.0 142.0 all-reduce.9
  393.9 67.2 all-gather.6
  507.6 135.5 all-reduce.11
